TPU v7x, 128 devices: a whole 4x4x4 slice. The times are simulated.
128 devices in a mesh: day: 32 (over z, x, core), pt: 4 (over y).
Axes of the slice: x: 4, y: 4, z: 4, core: 2. Of those that a mesh axis runs over, the one named last changes fastest.
Arguments:
- points: bfloat16 [32, 64, 2048], P('day', None, 'pt'), may hold values from -0.45 to 0.45
- cells: bfloat16 [32, 64, 8192], P('day', None, 'pt'), may hold values from -0.44921875 to 0.44921875
- clone_weight: float32 [32, 64, 2048], P('day', None, 'pt'), may hold values from 0.1 to 1
- potential: float32 [32, 2048], P('day', 'pt'), may hold values from 0.2 to 5
- support_count: int32 [32], P('day'), may hold values from 512 to 2048, as said below
- cell_count: int32 [32], P('day'), may hold values from 2048 to 8192, as said below
Outputs:
- forward_message: float32 [32, 64, 2048], P('day', None, 'pt')
- backward_message: float32 [32, 64, 2048], P('day', None, 'pt')
- fit_ratio: float32 [32, 2048], P('day', 'pt')
Inputs may be any that keep to these rules, and one draw needn't show every extreme that they name: Live support points of a day are its first support_count slots; some day has all 2048 slots live and some day has 512. Observed cells of a day are its first cell_count slots; some day fills all 8192 slots and some day has 2048.
All inputs are finite; a program needn't handle non-finite values.
Results may differ from a plain program's by a relative error of at most 0.0003.
Values may be sent and summed in bfloat16 or wider, within the bound.
A program may use at most 64 MiB of HBM per device.

v0:
```python
import jax
import jax.numpy as jnp
from jax import lax
from jax.sharding import PartitionSpec as P


def with_halo(cells, sides, width):
    for axis, dim in sides:
        count = lax.axis_size(axis)
        ends = count - 1
        head = lax.slice_in_dim(cells, 0, width, axis=dim)
        tail = lax.slice_in_dim(cells, cells.shape[dim] - width, cells.shape[dim], axis=dim)
        cells = jnp.concatenate(
            [
                lax.ppermute(tail, axis, [(i, (i + 1) % count) for i in range(ends)]),
                cells,
                lax.ppermute(head, axis, [((i + 1) % count, i) for i in range(ends)]),
            ],
            axis=dim,
        )
    return cells


def shifted(block, axis, distance):
    devices = range(lax.axis_size(axis))
    route = [(i - distance, i) for i in devices if i - distance in devices]
    return lax.ppermute(block, axis, route)


def norm_of(coords):
    wide = coords.astype(jnp.float32)
    return jnp.sum(wide * wide, axis=0)


def squared_dist(left_pts, left_norm, right_pts, right_norm):
    inner = lax.dot_general(
        left_pts, right_pts, (((0,), (0,)), ((), ())), preferred_element_type=jnp.float32
    )
    return left_norm[:, None] + right_norm[None, :] - 2.0 * inner


def shards(points, cells, clone_weight, potential, support_count, cell_count):
    pt_rank = lax.axis_index("pt")
    day_index = lax.axis_index("day")
    day_count = lax.axis_size("day")
    full_pts, full_clone, full_pot = (
        lax.all_gather(points.astype(jnp.float32), "pt", axis=2, tiled=True).astype(points.dtype),
        lax.all_gather(clone_weight, "pt", axis=2, tiled=True),
        lax.all_gather(potential, "pt", axis=1, tiled=True),
    )
    beside_all = with_halo(full_pts, (("day", 0),), 1)
    before_day = beside_all[0]
    after_day = beside_all[2]
    own_pts = points[0]
    per_device = own_pts.shape[1]
    support_total = full_pts.shape[2]
    clones = clone_weight.shape[1]
    weight = full_clone[0] * full_pot
    live_total = support_count[0].astype(jnp.float32)
    live_all = (jnp.arange(support_total, dtype=jnp.int32) < support_count[0]).astype(jnp.float32)
    live_own = lax.dynamic_slice_in_dim(live_all, pt_rank * per_device, per_device)
    own_norm = norm_of(own_pts)
    before_norm = norm_of(before_day)
    after_norm = norm_of(after_day)
    row_span = 512
    span_count = support_total // row_span

    def kernel_rows(source_pts, source_norm, block_index):
        offset = block_index * row_span
        source_rows = lax.dynamic_slice_in_dim(source_pts, offset, row_span, 1)
        norm_rows = lax.dynamic_slice_in_dim(source_norm, offset, row_span, 0)
        return jnp.exp(-squared_dist(source_rows, norm_rows, own_pts, own_norm)).astype(
            jnp.bfloat16
        )

    def contract(sent_rows, source_pts, source_norm):

        def add_rows(block_index, result):
            sent_part = lax.dynamic_slice_in_dim(sent_rows, block_index * row_span, row_span, 1)
            return result + jnp.dot(
                sent_part,
                kernel_rows(source_pts, source_norm, block_index),
                preferred_element_type=jnp.float32,
            )

        return lax.fori_loop(
            0, span_count, add_rows, jnp.zeros((sent_rows.shape[0], per_device), jnp.float32)
        )

    block_count = 4
    block_rows = clones // block_count
    steps_total = day_count + block_count - 1
    empty_rows = jnp.zeros((block_rows, per_device), jnp.float32)
    seed_rows = jnp.broadcast_to(live_own[None, :], (block_rows, per_device))

    def settle(piece_rows, full_rows, valid):
        column_sums = jnp.sum(full_rows * live_all[None, :], axis=1, keepdims=True)
        column_sums = jnp.where(valid, column_sums, 1.0)
        own_part = piece_rows * live_own[None, :] * live_total / column_sums
        whole_part = full_rows * live_all[None, :] * live_total / column_sums
        return (own_part, whole_part)

    def one_step(step_index, carried):
        forward_in, backward_in, forward_out, backward_out = carried
        forward_at = step_index - day_index
        forward_ok = (forward_at >= 0) & (forward_at < block_count)
        forward_block = jnp.clip(forward_at, 0, block_count - 1)
        backward_at = step_index - (day_count - 1 - day_index)
        backward_ok = (backward_at >= 0) & (backward_at < block_count)
        backward_block = jnp.clip(backward_at, 0, block_count - 1)
        forward_got = lax.cond(
            forward_ok & (day_index > 0),
            lambda: contract(forward_in, before_day, before_norm),
            lambda: empty_rows,
        )
        forward_piece = jnp.where(day_index == 0, seed_rows, forward_got)
        backward_got = lax.cond(
            backward_ok & (day_index < day_count - 1),
            lambda: contract(backward_in, after_day, after_norm),
            lambda: empty_rows,
        )
        backward_piece = jnp.where(day_index == day_count - 1, seed_rows, backward_got)
        forward_full, backward_full = (
            lax.all_gather(forward_piece, "pt", axis=1, tiled=True),
            lax.all_gather(backward_piece, "pt", axis=1, tiled=True),
        )
        forward_own, forward_all = settle(forward_piece, forward_full, forward_ok)
        backward_own, backward_all = settle(backward_piece, backward_full, backward_ok)
        forward_out = jnp.where(
            forward_ok,
            lax.dynamic_update_slice_in_dim(
                forward_out, forward_own, forward_block * block_rows, 0
            ),
            forward_out,
        )
        backward_out = jnp.where(
            backward_ok,
            lax.dynamic_update_slice_in_dim(
                backward_out, backward_own, backward_block * block_rows, 0
            ),
            backward_out,
        )
        forward_sent = (
            forward_all
            * lax.dynamic_slice_in_dim(weight, forward_block * block_rows, block_rows, 0)
        ).astype(jnp.bfloat16)
        backward_sent = (
            backward_all
            * lax.dynamic_slice_in_dim(weight, backward_block * block_rows, block_rows, 0)
        ).astype(jnp.bfloat16)
        forward_in = shifted(forward_sent, "day", 1)
        backward_in = shifted(backward_sent, "day", -1)
        return (forward_in, backward_in, forward_out, backward_out)

    start_in = jnp.zeros((block_rows, support_total), jnp.bfloat16)
    start_out = jnp.zeros((clones, per_device), jnp.float32)
    carried = lax.fori_loop(0, steps_total, one_step, (start_in, start_in, start_out, start_out))
    forward_out = carried[2]
    backward_out = carried[3]
    mass_own = (
        live_own * potential[0] * jnp.sum(forward_out * clone_weight[0] * backward_out, axis=0)
    )
    cell_total = cell_count[0]
    cell_total_f = cell_total.astype(jnp.float32)
    all_cells = lax.all_gather(cells, "pt", axis=2, tiled=True)[0]
    cell_slots = all_cells.shape[1]
    cell_norm = norm_of(all_cells)
    fit_span = 512
    fit_blocks = cell_slots // fit_span

    def fit_columns(block_index):
        offset = block_index * fit_span
        chosen = lax.dynamic_slice_in_dim(all_cells, offset, fit_span, 1)
        chosen_norm = lax.dynamic_slice_in_dim(cell_norm, offset, fit_span, 0)
        return jnp.exp(-squared_dist(own_pts, own_norm, chosen, chosen_norm))

    def density_part(block_index):
        return jnp.dot(mass_own, fit_columns(block_index), precision=lax.Precision.HIGHEST)

    partial_density = lax.map(density_part, jnp.arange(fit_blocks)).reshape(cell_slots)
    column_sums, mass_total = lax.psum((partial_density, jnp.sum(mass_own)), "pt")
    density = column_sums / mass_total
    cell_live = (jnp.arange(cell_slots, dtype=jnp.int32) < cell_total).astype(jnp.float32)
    inverse = cell_live / density

    def ratio_part(block_index, running):
        chosen_inverse = lax.dynamic_slice_in_dim(inverse, block_index * fit_span, fit_span, 0)
        return running + jnp.dot(
            fit_columns(block_index), chosen_inverse, precision=lax.Precision.HIGHEST
        )

    summed = lax.fori_loop(0, fit_blocks, ratio_part, jnp.zeros((per_device,), jnp.float32))
    fit_rows_out = live_own / cell_total_f * summed
    return (forward_out[None], backward_out[None], fit_rows_out[None])


def solution(mesh):
    in_specs = (
        P("day", None, "pt"),
        P("day", None, "pt"),
        P("day", None, "pt"),
        P("day", "pt"),
        P("day"),
        P("day"),
    )
    out_specs = (P("day", None, "pt"), P("day", None, "pt"), P("day", "pt"))
    return jax.shard_map(shards, mesh=mesh, in_specs=in_specs, out_specs=out_specs, check_vma=False)
```

profile of v0, /device:TPU:0, one launch (start us, length us, event | category | flops | bytes accessed | tf_op | source)
XLA Modules:
  0.0 1607.6 jit_solution(1951104666775304493)
XLA Ops:
  7.2 13.1 all_gather.28
  24.8 13.6 all_gather.29
  50.4 1437.5 %while.76 = (s32[]{:T(128)}, bf16[16,2048]{1,0:T(8,128)(2,1)S(1)}, bf16[16,2048]{1,0:T(8,128)(2,1)S(1)}, f32[64,512]{1,0:T(8,128)S(1)}, f32[64,512]{1,0:T(8,128)...) while((s32[]{:T(128)}, bf16[16,2048]{1,0:T(8,128)(2,1)S(1)}, ...), condition=%wide.region_14.15_spmd.clone.clone, body=%wide.region_3.14_spmd.clone.clone.sunk | while | flops 87085088 | bytes 2573997 | solution.py:157
  85.6 12.0 all_gather.38
  121.1 12.0 all_gather.38
  161.5 12.0 all_gather.38
  243.1 12.0 all_gather.38
  283.9 12.0 all_gather.38
  318.3 12.0 all_gather.38
  352.6 12.0 all_gather.38
  389.2 12.0 all_gather.38
  423.5 12.0 all_gather.38
  496.4 12.0 all_gather.38
  530.8 12.0 all_gather.38
  569.9 12.0 all_gather.38
  597.5 13.3 collective-permute-done.1
  649.3 12.0 all_gather.38
  685.8 12.0 all_gather.38
  722.3 12.0 all_gather.38
  822.8 18.5 %collective-permute-done.1 = bf16[16,2048]{1,0:T(8,128)(2,1)S(1)} collective-permute-done((bf16[16,2048]{1,0:T(8,128)(2,1)S(1)}, bf16[16,2048]{1,0:T(8,128)(2,1)S(1)}, u32[]{:S(2)}, u32[]{:S(2)}) %collective-permute-start.1) | collective-permute-done | bytes 65568 | tf_op jit(solution)/shard_map/while/body/eval_jaxpr/ppermute | solution.py:27
  871.0 13.2 collective-permute-done.1
  913.8 17.7 %collective-permute-done.1 = bf16[16,2048]{1,0:T(8,128)(2,1)S(1)} collective-permute-done((bf16[16,2048]{1,0:T(8,128)(2,1)S(1)}, bf16[16,2048]{1,0:T(8,128)(2,1)S(1)}, u32[]{:S(2)}, u32[]{:S(2)}) %collective-permute-start.1) | collective-permute-done | bytes 65568 | tf_op jit(solution)/shard_map/while/body/eval_jaxpr/ppermute | solution.py:27
  961.2 26.2 %collective-permute-done.1 = bf16[16,2048]{1,0:T(8,128)(2,1)S(1)} collective-permute-done((bf16[16,2048]{1,0:T(8,128)(2,1)S(1)}, bf16[16,2048]{1,0:T(8,128)(2,1)S(1)}, u32[]{:S(2)}, u32[]{:S(2)}) %collective-permute-start.1) | collective-permute-done | bytes 65568 | tf_op jit(solution)/shard_map/while/body/eval_jaxpr/ppermute | solution.py:27
  1016.9 19.6 %collective-permute-done.1 = bf16[16,2048]{1,0:T(8,128)(2,1)S(1)} collective-permute-done((bf16[16,2048]{1,0:T(8,128)(2,1)S(1)}, bf16[16,2048]{1,0:T(8,128)(2,1)S(1)}, u32[]{:S(2)}, u32[]{:S(2)}) %collective-permute-start.1) | collective-permute-done | bytes 65568 | tf_op jit(solution)/shard_map/while/body/eval_jaxpr/ppermute | solution.py:27
  1066.2 26.1 %collective-permute-done.1 = bf16[16,2048]{1,0:T(8,128)(2,1)S(1)} collective-permute-done((bf16[16,2048]{1,0:T(8,128)(2,1)S(1)}, bf16[16,2048]{1,0:T(8,128)(2,1)S(1)}, u32[]{:S(2)}, u32[]{:S(2)}) %collective-permute-start.1) | collective-permute-done | bytes 65568 | tf_op jit(solution)/shard_map/while/body/eval_jaxpr/ppermute | solution.py:27
  1121.9 19.9 %collective-permute-done.1 = bf16[16,2048]{1,0:T(8,128)(2,1)S(1)} collective-permute-done((bf16[16,2048]{1,0:T(8,128)(2,1)S(1)}, bf16[16,2048]{1,0:T(8,128)(2,1)S(1)}, u32[]{:S(2)}, u32[]{:S(2)}) %collective-permute-start.1) | collective-permute-done | bytes 65568 | tf_op jit(solution)/shard_map/while/body/eval_jaxpr/ppermute | solution.py:27
  1171.4 19.7 %collective-permute-done.1 = bf16[16,2048]{1,0:T(8,128)(2,1)S(1)} collective-permute-done((bf16[16,2048]{1,0:T(8,128)(2,1)S(1)}, bf16[16,2048]{1,0:T(8,128)(2,1)S(1)}, u32[]{:S(2)}, u32[]{:S(2)}) %collective-permute-start.1) | collective-permute-done | bytes 65568 | tf_op jit(solution)/shard_map/while/body/eval_jaxpr/ppermute | solution.py:27
  1220.8 19.8 %collective-permute-done.1 = bf16[16,2048]{1,0:T(8,128)(2,1)S(1)} collective-permute-done((bf16[16,2048]{1,0:T(8,128)(2,1)S(1)}, bf16[16,2048]{1,0:T(8,128)(2,1)S(1)}, u32[]{:S(2)}, u32[]{:S(2)}) %collective-permute-start.1) | collective-permute-done | bytes 65568 | tf_op jit(solution)/shard_map/while/body/eval_jaxpr/ppermute | solution.py:27
  1270.1 19.7 %collective-permute-done.1 = bf16[16,2048]{1,0:T(8,128)(2,1)S(1)} collective-permute-done((bf16[16,2048]{1,0:T(8,128)(2,1)S(1)}, bf16[16,2048]{1,0:T(8,128)(2,1)S(1)}, u32[]{:S(2)}, u32[]{:S(2)}) %collective-permute-start.1) | collective-permute-done | bytes 65568 | tf_op jit(solution)/shard_map/while/body/eval_jaxpr/ppermute | solution.py:27
  1490.1 52.7 %while.74 = (s32[]{:T(128)}, f32[16,512]{1,0:T(8,128)S(1)}, f32[512]{0:T(512)S(1)}, s32[16]{0:T(128)S(1)}, f32[8192]{0:T(1024)S(1)}, /*index=5*/bf16[64,8192]{1,...) while((s32[]{:T(128)}, f32[16,512]{1,0:T(8,128)S(1)}, ...), condition=%wide.region_20.21_spmd, body=%wide.region_19.20_spmd.sunk | while | flops 37748740 | bytes 2244795 | solution.py:180
  1542.9 18.0 %all-reduce = (f32[8192]{0:T(1024)S(1)}, f32[]{:T(128)}) all-reduce(f32[8192]{0:T(1024)S(1)} %bitcast.96, f32[]{:T(128)} %get-tuple-element.1099), channel_id=1, replica_groups=mesh['day'=32,'pt'=4] {'pt'}, use_global_device_ids=true, to_apply=%region_21.22 | all-reduce | flops 8193 | bytes 65544 | tf_op jit(solution)/shard_map/psum | solution.py:181
  1561.6 38.6 %while.75 = (s32[]{:T(128)}, f32[512]{0:T(512)S(1)}, f32[512]{0:T(512)S(1)}, f32[8192]{0:T(1024)S(1)}, bf16[64,8192]{1,0:T(8,128)(2,1)}, /*index=5*/bf16[64,512]...) while((s32[]{:T(128)}, f32[512]{0:T(512)S(1)}, ...), condition=%wide.region_23.24_spmd.clone, body=%wide.region_22.23_spmd.clone.sunk | while | flops 37749764 | bytes 2250929 | solution.py:192
  (766 shorter events, 1237.4 us)
Async XLA Ops:
  7.2 1481.4 %all-gather.2.cloned.1.call-start = ((), (), s32[]{:S(2)}) async-start(), calls=%async_computation | async-start | bytes 1310720 | tf_op jit(solution)/shard_map/all_gather | solution.py:165
  20.3 29.9 %collective-permute-start.3 = (bf16[1,64,2048]{2,1,0:T(8,128)(2,1)S(1)}, bf16[1,64,2048]{2,1,0:T(8,128)(2,1)S(1)}, u32[]{:S(2)}, u32[]{:S(2)}) collective-permute-start(bf16[1,64,2048]{2,1,0:T(8,128)(2,1)S(1)} %all_gather.28), channel_id=1, source_target_pairs={{4,0},{8,4},{12,8},{16,12},{20,16},{24,20},{28,24},{32,28},{36,32}... | collective-permute-start | bytes 786440 | tf_op jit(solution)/shard_map/ppermute | solution.py:17
  21.7 28.6 %collective-permute-start.2 = (bf16[1,64,2048]{2,1,0:T(8,128)(2,1)S(1)}, bf16[1,64,2048]{2,1,0:T(8,128)(2,1)S(1)}, u32[]{:S(2)}, u32[]{:S(2)}) collective-permute-start(bf16[1,64,2048]{2,1,0:T(8,128)(2,1)S(1)} %all_gather.28), channel_id=1, source_target_pairs={{0,4},{4,8},{8,12},{12,16},{16,20},{20,24},{24,28},{28,32},{32,36}... | collective-permute-start | bytes 786440 | tf_op jit(solution)/shard_map/ppermute | solution.py:15
  110.5 6.9 collective-permute-start
  146.0 6.5 collective-permute-start
  151.2 8.3 collective-permute-start.1
  186.4 6.9 collective-permute-start
  191.9 8.4 collective-permute-start.1
  227.2 6.9 collective-permute-start
  232.7 8.4 collective-permute-start.1
  269.3 12.6 collective-permute-start.1
  378.9 8.3 collective-permute-start.1
  484.1 10.3 collective-permute-start.1
  557.0 10.9 collective-permute-start.1
  596.1 14.7 collective-permute-start.1
  639.0 8.3 collective-permute-start.1
  675.5 8.3 collective-permute-start.1
  712.0 8.3 collective-permute-start.1
  748.5 8.3 collective-permute-start.1
  784.9 8.3 collective-permute-start.1
  821.4 19.9 %collective-permute-start.1 = (bf16[16,2048]{1,0:T(8,128)(2,1)S(1)}, bf16[16,2048]{1,0:T(8,128)(2,1)S(1)}, u32[]{:S(2)}, u32[]{:S(2)}) collective-permute-start(bf16[16,2048]{1,0:T(8,128)(2,1)S(1)} %get-tuple-element.1417), channel_id=1, source_target_pairs={{4,0},{8,4},{12,8},{16,12},{20,16},{24,20},{28,24},{32,28},{36,32}... | collective-permute-start | bytes 196616 | tf_op jit(solution)/shard_map/while/body/eval_jaxpr/ppermute | solution.py:27
  869.6 14.6 collective-permute-start.1
  912.4 19.1 %collective-permute-start.1 = (bf16[16,2048]{1,0:T(8,128)(2,1)S(1)}, bf16[16,2048]{1,0:T(8,128)(2,1)S(1)}, u32[]{:S(2)}, u32[]{:S(2)}) collective-permute-start(bf16[16,2048]{1,0:T(8,128)(2,1)S(1)} %get-tuple-element.1417), channel_id=1, source_target_pairs={{4,0},{8,4},{12,8},{16,12},{20,16},{24,20},{28,24},{32,28},{36,32}... | collective-permute-start | bytes 196616 | tf_op jit(solution)/shard_map/while/body/eval_jaxpr/ppermute | solution.py:27
  959.8 27.6 %collective-permute-start.1 = (bf16[16,2048]{1,0:T(8,128)(2,1)S(1)}, bf16[16,2048]{1,0:T(8,128)(2,1)S(1)}, u32[]{:S(2)}, u32[]{:S(2)}) collective-permute-start(bf16[16,2048]{1,0:T(8,128)(2,1)S(1)} %get-tuple-element.1417), channel_id=1, source_target_pairs={{4,0},{8,4},{12,8},{16,12},{20,16},{24,20},{28,24},{32,28},{36,32}... | collective-permute-start | bytes 196616 | tf_op jit(solution)/shard_map/while/body/eval_jaxpr/ppermute | solution.py:27
  1015.5 21.0 %collective-permute-start.1 = (bf16[16,2048]{1,0:T(8,128)(2,1)S(1)}, bf16[16,2048]{1,0:T(8,128)(2,1)S(1)}, u32[]{:S(2)}, u32[]{:S(2)}) collective-permute-start(bf16[16,2048]{1,0:T(8,128)(2,1)S(1)} %get-tuple-element.1417), channel_id=1, source_target_pairs={{4,0},{8,4},{12,8},{16,12},{20,16},{24,20},{28,24},{32,28},{36,32}... | collective-permute-start | bytes 196616 | tf_op jit(solution)/shard_map/while/body/eval_jaxpr/ppermute | solution.py:27
  1064.8 27.5 %collective-permute-start.1 = (bf16[16,2048]{1,0:T(8,128)(2,1)S(1)}, bf16[16,2048]{1,0:T(8,128)(2,1)S(1)}, u32[]{:S(2)}, u32[]{:S(2)}) collective-permute-start(bf16[16,2048]{1,0:T(8,128)(2,1)S(1)} %get-tuple-element.1417), channel_id=1, source_target_pairs={{4,0},{8,4},{12,8},{16,12},{20,16},{24,20},{28,24},{32,28},{36,32}... | collective-permute-start | bytes 196616 | tf_op jit(solution)/shard_map/while/body/eval_jaxpr/ppermute | solution.py:27
  1120.5 21.3 %collective-permute-start.1 = (bf16[16,2048]{1,0:T(8,128)(2,1)S(1)}, bf16[16,2048]{1,0:T(8,128)(2,1)S(1)}, u32[]{:S(2)}, u32[]{:S(2)}) collective-permute-start(bf16[16,2048]{1,0:T(8,128)(2,1)S(1)} %get-tuple-element.1417), channel_id=1, source_target_pairs={{4,0},{8,4},{12,8},{16,12},{20,16},{24,20},{28,24},{32,28},{36,32}... | collective-permute-start | bytes 196616 | tf_op jit(solution)/shard_map/while/body/eval_jaxpr/ppermute | solution.py:27
  1170.0 21.2 %collective-permute-start.1 = (bf16[16,2048]{1,0:T(8,128)(2,1)S(1)}, bf16[16,2048]{1,0:T(8,128)(2,1)S(1)}, u32[]{:S(2)}, u32[]{:S(2)}) collective-permute-start(bf16[16,2048]{1,0:T(8,128)(2,1)S(1)} %get-tuple-element.1417), channel_id=1, source_target_pairs={{4,0},{8,4},{12,8},{16,12},{20,16},{24,20},{28,24},{32,28},{36,32}... | collective-permute-start | bytes 196616 | tf_op jit(solution)/shard_map/while/body/eval_jaxpr/ppermute | solution.py:27
  1219.4 21.2 %collective-permute-start.1 = (bf16[16,2048]{1,0:T(8,128)(2,1)S(1)}, bf16[16,2048]{1,0:T(8,128)(2,1)S(1)}, u32[]{:S(2)}, u32[]{:S(2)}) collective-permute-start(bf16[16,2048]{1,0:T(8,128)(2,1)S(1)} %get-tuple-element.1417), channel_id=1, source_target_pairs={{4,0},{8,4},{12,8},{16,12},{20,16},{24,20},{28,24},{32,28},{36,32}... | collective-permute-start | bytes 196616 | tf_op jit(solution)/shard_map/while/body/eval_jaxpr/ppermute | solution.py:27
  1268.7 21.1 %collective-permute-start.1 = (bf16[16,2048]{1,0:T(8,128)(2,1)S(1)}, bf16[16,2048]{1,0:T(8,128)(2,1)S(1)}, u32[]{:S(2)}, u32[]{:S(2)}) collective-permute-start(bf16[16,2048]{1,0:T(8,128)(2,1)S(1)} %get-tuple-element.1417), channel_id=1, source_target_pairs={{4,0},{8,4},{12,8},{16,12},{20,16},{24,20},{28,24},{32,28},{36,32}... | collective-permute-start | bytes 196616 | tf_op jit(solution)/shard_map/while/body/eval_jaxpr/ppermute | solution.py:27
  1316.8 6.9 collective-permute-start
  1322.3 8.5 collective-permute-start.1
  (46 other events, 1641.3 us)
Sparse Core Ops, SparseCore 0:
  24.9 26.1 all-gather.1
where the time goes:
time: 1620 us; the launch traced here: 1610 us
  blocking collectives  894 us (55%)
  waiting for transfers between devices  355 us (22%)
  starting transfers between devices  116 us (7%)
  matrix products  92 us (6%)
  other arithmetic  65.3 us (4%)
  local copies, waits for them, and re-layouts  56.8 us (4%)
    all_gather x35, blocking collectives, one_step(): lax.all_gather(backward_piece, 'pt', axis=1, tiled=True)  420 us
    all_gather x35, blocking collectives, one_step(): lax.all_gather(forward_piece, 'pt', axis=1, tiled=True)  419 us
    ppermute x70, waiting for transfers between devices, shifted(): return lax.ppermute(block, axis, route)  355 us
    ppermute x70, starting transfers between devices, shifted(): return lax.ppermute(block, axis, route)  111 us
    another operation x66, local copies, waits for them, and re-layouts  40.7 us
    dot_general x32, matrix products, squared_dist(): lax.dot_general(left_pts, right_pts, (((0,), (0,)), ((), ())), preferred_...  39 us
  transfers between devices with their start and end apart: 73, of which 35 were waited for; matrix products, arithmetic and copies ran while one was open for 8% of the time, Pallas kernels for 0%

commit v1 on v0

--- a/solution.py
+++ b/solution.py
@@ -2,6 +2,18 @@
 import jax.numpy as jnp
 from jax import lax
 from jax.sharding import PartitionSpec as P
+
+
+def gather_by_bits(value, axis, dim):
+    ways, here, hop = (lax.axis_size(axis), lax.axis_index(axis), value.shape[dim])
+    line, have = (value, 1)
+    while have < ways:
+        line = jnp.concatenate(
+            [line, lax.ppermute(line, axis, [(d, (d - have) % ways) for d in range(ways)])],
+            axis=dim,
+        )
+        have = 2 * have
+    return jnp.roll(line, here * hop, axis=dim)
 
 
 def with_halo(cells, sides, width):
@@ -122,7 +134,7 @@
         backward_piece = jnp.where(day_index == day_count - 1, seed_rows, backward_got)
         forward_full, backward_full = (
             lax.all_gather(forward_piece, "pt", axis=1, tiled=True),
-            lax.all_gather(backward_piece, "pt", axis=1, tiled=True),
+            gather_by_bits(backward_piece, "pt", 1),
         )
         forward_own, forward_all = settle(forward_piece, forward_full, forward_ok)
         backward_own, backward_all = settle(backward_piece, backward_full, backward_ok)

time: 1620 us -> 1440 us (0.89)
  blocking collectives: 894 us -> 476 us
  waiting for transfers between devices: 355 us -> 495 us
  starting transfers between devices: 116 us -> 220 us
    all_gather x35 -> x0, blocking collectives: 420 us -> none  [one_step(): lax.all_gather(backward_piece, 'pt', axis=1, tiled=True)]
    ppermute x0 -> x70, waiting for transfers between devices: none -> 152 us  [gather_by_bits(): lax.ppermute(line, axis, [(d, (d - have) % ways) for d in range(ways)])]
    ppermute x0 -> x70, starting transfers between devices: none -> 93.1 us  [gather_by_bits(): lax.ppermute(line, axis, [(d, (d - have) % ways) for d in range(ways)])]
    while x0 -> x35, other arithmetic: none -> 26.9 us
    select_n x35 -> x0, other arithmetic: 26.9 us -> none  [one_step(): jnp.where(day_index == day_count - 1, seed_rows, backward_got)]
  transfers between devices with their start and end apart: 73 -> 143, of which waited for: 35 -> 70; matrix products, arithmetic and copies ran while one was open for 8% -> 9% of each run, Pallas kernels for 0% -> 0%
where the time goes in v1:
time: 1440 us
  waiting for transfers between devices  495 us (34%)
  blocking collectives  476 us (33%)
  starting transfers between devices  220 us (15%)
  matrix products  92 us (6%)
  other arithmetic  65.6 us (5%)
  local copies, waits for them, and re-layouts  57.7 us (4%)
  between operations  15.5 us (1%)
  loops' own time  14.6 us (1%)
    all_gather x35, blocking collectives, one_step(): lax.all_gather(forward_piece, 'pt', axis=1, tiled=True)  423 us
    ppermute x70, waiting for transfers between devices, shifted(): return lax.ppermute(block, axis, route)  343 us
    ppermute x70, waiting for transfers between devices, gather_by_bits(): lax.ppermute(line, axis, [(d, (d - have) % ways) for d in range(ways)])  152 us
    ppermute x70, starting transfers between devices, shifted(): return lax.ppermute(block, axis, route)  123 us
    ppermute x70, starting transfers between devices, gather_by_bits(): lax.ppermute(line, axis, [(d, (d - have) % ways) for d in range(ways)])  93.1 us
    another operation x66, local copies, waits for them, and re-layouts  40.7 us
    dot_general x32, matrix products, squared_dist(): lax.dot_general(left_pts, right_pts, (((0,), (0,)), ((), ())), preferred_...  39 us
  transfers between devices with their start and end apart: 143, of which 70 were waited for; matrix products, arithmetic and copies ran while one was open for 9% of the time, Pallas kernels for 0%

profile of v1, /device:TPU:0, one launch (start us, length us, event | category | flops | bytes accessed | tf_op | source)
XLA Modules:
  0.0 1436.1 jit_solution(11165994091460561351)
XLA Ops:
  7.2 13.1 all_gather.22
  24.8 13.6 all_gather.23
  50.4 1268.4 %while.77 = (s32[]{:T(128)}, bf16[16,2048]{1,0:T(8,128)(2,1)S(1)}, bf16[16,2048]{1,0:T(8,128)(2,1)S(1)}, f32[64,512]{1,0:T(8,128)S(1)}, f32[64,512]{1,0:T(8,128)...) while((s32[]{:T(128)}, bf16[16,2048]{1,0:T(8,128)(2,1)S(1)}, ...), condition=%wide.region_14.15_spmd.clone.clone, body=%wide.region_3.14_spmd.clone.clone.sunk | while | flops 87101472 | bytes 3426280 | solution.py:169
  222.4 12.1 all_gather.29
  258.5 12.1 all_gather.29
  288.2 12.1 all_gather.29
  318.0 12.1 all_gather.29
  350.9 12.1 all_gather.29
  381.2 12.1 all_gather.29
  410.5 12.1 all_gather.29
  443.9 12.1 all_gather.29
  473.4 12.1 all_gather.29
  506.7 12.1 all_gather.29
  527.7 13.2 collective-permute-done.3
  544.8 12.1 all_gather.29
  576.3 12.1 all_gather.29
  608.6 12.1 all_gather.29
  639.5 12.1 all_gather.29
  723.8 16.3 %collective-permute-done.3 = bf16[16,2048]{1,0:T(8,128)(2,1)S(1)} collective-permute-done((bf16[16,2048]{1,0:T(8,128)(2,1)S(1)}, bf16[16,2048]{1,0:T(8,128)(2,1)S(1)}, u32[]{:S(2)}, u32[]{:S(2)}) %collective-permute-start.3) | collective-permute-done | bytes 65568 | tf_op jit(solution)/shard_map/while/body/eval_jaxpr/ppermute | solution.py:39
  764.2 12.9 collective-permute-done.3
  802.5 17.8 %collective-permute-done.3 = bf16[16,2048]{1,0:T(8,128)(2,1)S(1)} collective-permute-done((bf16[16,2048]{1,0:T(8,128)(2,1)S(1)}, bf16[16,2048]{1,0:T(8,128)(2,1)S(1)}, u32[]{:S(2)}, u32[]{:S(2)}) %collective-permute-start.3) | collective-permute-done | bytes 65568 | tf_op jit(solution)/shard_map/while/body/eval_jaxpr/ppermute | solution.py:39
  844.3 26.4 %collective-permute-done.3 = bf16[16,2048]{1,0:T(8,128)(2,1)S(1)} collective-permute-done((bf16[16,2048]{1,0:T(8,128)(2,1)S(1)}, bf16[16,2048]{1,0:T(8,128)(2,1)S(1)}, u32[]{:S(2)}, u32[]{:S(2)}) %collective-permute-start.3) | collective-permute-done | bytes 65568 | tf_op jit(solution)/shard_map/while/body/eval_jaxpr/ppermute | solution.py:39
  896.1 20.0 %collective-permute-done.3 = bf16[16,2048]{1,0:T(8,128)(2,1)S(1)} collective-permute-done((bf16[16,2048]{1,0:T(8,128)(2,1)S(1)}, bf16[16,2048]{1,0:T(8,128)(2,1)S(1)}, u32[]{:S(2)}, u32[]{:S(2)}) %collective-permute-start.3) | collective-permute-done | bytes 65568 | tf_op jit(solution)/shard_map/while/body/eval_jaxpr/ppermute | solution.py:39
  940.6 25.9 %collective-permute-done.3 = bf16[16,2048]{1,0:T(8,128)(2,1)S(1)} collective-permute-done((bf16[16,2048]{1,0:T(8,128)(2,1)S(1)}, bf16[16,2048]{1,0:T(8,128)(2,1)S(1)}, u32[]{:S(2)}, u32[]{:S(2)}) %collective-permute-start.3) | collective-permute-done | bytes 65568 | tf_op jit(solution)/shard_map/while/body/eval_jaxpr/ppermute | solution.py:39
  991.9 20.0 %collective-permute-done.3 = bf16[16,2048]{1,0:T(8,128)(2,1)S(1)} collective-permute-done((bf16[16,2048]{1,0:T(8,128)(2,1)S(1)}, bf16[16,2048]{1,0:T(8,128)(2,1)S(1)}, u32[]{:S(2)}, u32[]{:S(2)}) %collective-permute-start.3) | collective-permute-done | bytes 65568 | tf_op jit(solution)/shard_map/while/body/eval_jaxpr/ppermute | solution.py:39
  1035.6 19.8 %collective-permute-done.3 = bf16[16,2048]{1,0:T(8,128)(2,1)S(1)} collective-permute-done((bf16[16,2048]{1,0:T(8,128)(2,1)S(1)}, bf16[16,2048]{1,0:T(8,128)(2,1)S(1)}, u32[]{:S(2)}, u32[]{:S(2)}) %collective-permute-start.3) | collective-permute-done | bytes 65568 | tf_op jit(solution)/shard_map/while/body/eval_jaxpr/ppermute | solution.py:39
  1081.6 18.8 %collective-permute-done.3 = bf16[16,2048]{1,0:T(8,128)(2,1)S(1)} collective-permute-done((bf16[16,2048]{1,0:T(8,128)(2,1)S(1)}, bf16[16,2048]{1,0:T(8,128)(2,1)S(1)}, u32[]{:S(2)}, u32[]{:S(2)}) %collective-permute-start.3) | collective-permute-done | bytes 65568 | tf_op jit(solution)/shard_map/while/body/eval_jaxpr/ppermute | solution.py:39
  1103.6 12.2 all_gather.29
  1127.8 16.5 %collective-permute-done.3 = bf16[16,2048]{1,0:T(8,128)(2,1)S(1)} collective-permute-done((bf16[16,2048]{1,0:T(8,128)(2,1)S(1)}, bf16[16,2048]{1,0:T(8,128)(2,1)S(1)}, u32[]{:S(2)}, u32[]{:S(2)}) %collective-permute-start.3) | collective-permute-done | bytes 65568 | tf_op jit(solution)/shard_map/while/body/eval_jaxpr/ppermute | solution.py:39
  1321.0 52.7 %while.75 = (s32[]{:T(128)}, f32[16,512]{1,0:T(8,128)S(1)}, f32[512]{0:T(512)S(1)}, s32[16]{0:T(128)S(1)}, f32[8192]{0:T(1024)S(1)}, /*index=5*/bf16[64,8192]{1,...) while((s32[]{:T(128)}, f32[16,512]{1,0:T(8,128)S(1)}, ...), condition=%wide.region_20.21_spmd, body=%wide.region_19.20_spmd.sunk | while | flops 37748740 | bytes 2244795 | solution.py:192
  1373.7 15.6 %all-reduce = (f32[8192]{0:T(1024)S(1)}, f32[]{:T(128)}) all-reduce(f32[8192]{0:T(1024)S(1)} %bitcast.96, f32[]{:T(128)} %get-tuple-element.1170), channel_id=1, replica_groups=mesh['day'=32,'pt'=4] {'pt'}, use_global_device_ids=true, to_apply=%region_21.22 | all-reduce | flops 8193 | bytes 65544 | tf_op jit(solution)/shard_map/psum | solution.py:193
  1390.0 38.6 %while.76 = (s32[]{:T(128)}, f32[512]{0:T(512)S(1)}, f32[512]{0:T(512)S(1)}, f32[8192]{0:T(1024)S(1)}, bf16[64,8192]{1,0:T(8,128)(2,1)}, /*index=5*/bf16[64,512]...) while((s32[]{:T(128)}, f32[512]{0:T(512)S(1)}, ...), condition=%wide.region_23.24_spmd.clone, body=%wide.region_22.23_spmd.clone.sunk | while | flops 37749764 | bytes 2250929 | solution.py:204
  (1081 shorter events, 1071.1 us)
Async XLA Ops:
  7.2 1312.3 %all-gather.2.cloned.1.call-start = ((), (), s32[]{:S(2)}) async-start(), calls=%async_computation | async-start | bytes 1310720 | tf_op jit(solution)/shard_map/all_gather | solution.py:177
  20.3 29.9 %collective-permute-start.5 = (bf16[1,64,2048]{2,1,0:T(8,128)(2,1)S(1)}, bf16[1,64,2048]{2,1,0:T(8,128)(2,1)S(1)}, u32[]{:S(2)}, u32[]{:S(2)}) collective-permute-start(bf16[1,64,2048]{2,1,0:T(8,128)(2,1)S(1)} %all_gather.22), channel_id=1, source_target_pairs={{4,0},{8,4},{12,8},{16,12},{20,16},{24,20},{28,24},{32,28},{36,32}... | collective-permute-start | bytes 786440 | tf_op jit(solution)/shard_map/ppermute | solution.py:29
  21.7 28.6 %collective-permute-start.4 = (bf16[1,64,2048]{2,1,0:T(8,128)(2,1)S(1)}, bf16[1,64,2048]{2,1,0:T(8,128)(2,1)S(1)}, u32[]{:S(2)}, u32[]{:S(2)}) collective-permute-start(bf16[1,64,2048]{2,1,0:T(8,128)(2,1)S(1)} %all_gather.22), channel_id=1, source_target_pairs={{0,4},{4,8},{8,12},{12,16},{16,20},{20,24},{24,28},{28,32},{32,36}... | collective-permute-start | bytes 786440 | tf_op jit(solution)/shard_map/ppermute | solution.py:27
  52.5 15.0 %collective-permute-start = (f32[16,512]{1,0:T(8,128)S(1)}, f32[16,512]{1,0:T(8,128)S(1)}, u32[]{:S(2)}, u32[]{:S(2)}) collective-permute-start(f32[16,512]{1,0:T(8,128)S(1)} %get-tuple-element.1482), channel_id=1, source_target_pairs={{0,3},{1,0},{2,1},{3,2},{4,7},{5,4},{6,5},{7,6},{8,11},{9,8},{10,9... | collective-permute-start | bytes 98312 | tf_op jit(solution)/shard_map/while/body/eval_jaxpr/ppermute | solution.py:12
  113.6 14.1 collective-permute-start
  184.8 14.1 collective-permute-start
  256.4 14.2 collective-permute-start
  316.0 14.1 collective-permute-start
  379.1 14.2 collective-permute-start
  471.5 14.0 collective-permute-start
  504.8 14.0 collective-permute-start
  526.3 14.6 %collective-permute-start.3 = (bf16[16,2048]{1,0:T(8,128)(2,1)S(1)}, bf16[16,2048]{1,0:T(8,128)(2,1)S(1)}, u32[]{:S(2)}, u32[]{:S(2)}) collective-permute-start(bf16[16,2048]{1,0:T(8,128)(2,1)S(1)} %get-tuple-element.1489), channel_id=1, source_target_pairs={{4,0},{8,4},{12,8},{16,12},{20,16},{24,20},{28,24},{32,28},{36,32}... | collective-permute-start | bytes 196616 | tf_op jit(solution)/shard_map/while/body/eval_jaxpr/ppermute | solution.py:39
  542.9 14.0 collective-permute-start
  606.2 14.6 %collective-permute-start = (f32[16,512]{1,0:T(8,128)S(1)}, f32[16,512]{1,0:T(8,128)S(1)}, u32[]{:S(2)}, u32[]{:S(2)}) collective-permute-start(f32[16,512]{1,0:T(8,128)S(1)} %get-tuple-element.1482), channel_id=1, source_target_pairs={{0,3},{1,0},{2,1},{3,2},{4,7},{5,4},{6,5},{7,6},{8,11},{9,8},{10,9... | collective-permute-start | bytes 98312 | tf_op jit(solution)/shard_map/while/body/eval_jaxpr/ppermute | solution.py:12
  669.7 14.5 %collective-permute-start = (f32[16,512]{1,0:T(8,128)S(1)}, f32[16,512]{1,0:T(8,128)S(1)}, u32[]{:S(2)}, u32[]{:S(2)}) collective-permute-start(f32[16,512]{1,0:T(8,128)S(1)} %get-tuple-element.1482), channel_id=1, source_target_pairs={{0,3},{1,0},{2,1},{3,2},{4,7},{5,4},{6,5},{7,6},{8,11},{9,8},{10,9... | collective-permute-start | bytes 98312 | tf_op jit(solution)/shard_map/while/body/eval_jaxpr/ppermute | solution.py:12
  722.4 17.7 %collective-permute-start.3 = (bf16[16,2048]{1,0:T(8,128)(2,1)S(1)}, bf16[16,2048]{1,0:T(8,128)(2,1)S(1)}, u32[]{:S(2)}, u32[]{:S(2)}) collective-permute-start(bf16[16,2048]{1,0:T(8,128)(2,1)S(1)} %get-tuple-element.1489), channel_id=1, source_target_pairs={{4,0},{8,4},{12,8},{16,12},{20,16},{24,20},{28,24},{32,28},{36,32}... | collective-permute-start | bytes 196616 | tf_op jit(solution)/shard_map/while/body/eval_jaxpr/ppermute | solution.py:39
  762.8 14.3 collective-permute-start.3
  779.1 14.5 %collective-permute-start = (f32[16,512]{1,0:T(8,128)S(1)}, f32[16,512]{1,0:T(8,128)S(1)}, u32[]{:S(2)}, u32[]{:S(2)}) collective-permute-start(f32[16,512]{1,0:T(8,128)S(1)} %get-tuple-element.1482), channel_id=1, source_target_pairs={{0,3},{1,0},{2,1},{3,2},{4,7},{5,4},{6,5},{7,6},{8,11},{9,8},{10,9... | collective-permute-start | bytes 98312 | tf_op jit(solution)/shard_map/while/body/eval_jaxpr/ppermute | solution.py:12
  801.1 19.2 %collective-permute-start.3 = (bf16[16,2048]{1,0:T(8,128)(2,1)S(1)}, bf16[16,2048]{1,0:T(8,128)(2,1)S(1)}, u32[]{:S(2)}, u32[]{:S(2)}) collective-permute-start(bf16[16,2048]{1,0:T(8,128)(2,1)S(1)} %get-tuple-element.1489), channel_id=1, source_target_pairs={{4,0},{8,4},{12,8},{16,12},{20,16},{24,20},{28,24},{32,28},{36,32}... | collective-permute-start | bytes 196616 | tf_op jit(solution)/shard_map/while/body/eval_jaxpr/ppermute | solution.py:39
  842.9 27.8 %collective-permute-start.3 = (bf16[16,2048]{1,0:T(8,128)(2,1)S(1)}, bf16[16,2048]{1,0:T(8,128)(2,1)S(1)}, u32[]{:S(2)}, u32[]{:S(2)}) collective-permute-start(bf16[16,2048]{1,0:T(8,128)(2,1)S(1)} %get-tuple-element.1489), channel_id=1, source_target_pairs={{4,0},{8,4},{12,8},{16,12},{20,16},{24,20},{28,24},{32,28},{36,32}... | collective-permute-start | bytes 196616 | tf_op jit(solution)/shard_map/while/body/eval_jaxpr/ppermute | solution.py:39
  872.7 14.6 %collective-permute-start = (f32[16,512]{1,0:T(8,128)S(1)}, f32[16,512]{1,0:T(8,128)S(1)}, u32[]{:S(2)}, u32[]{:S(2)}) collective-permute-start(f32[16,512]{1,0:T(8,128)S(1)} %get-tuple-element.1482), channel_id=1, source_target_pairs={{0,3},{1,0},{2,1},{3,2},{4,7},{5,4},{6,5},{7,6},{8,11},{9,8},{10,9... | collective-permute-start | bytes 98312 | tf_op jit(solution)/shard_map/while/body/eval_jaxpr/ppermute | solution.py:12
  894.7 21.4 %collective-permute-start.3 = (bf16[16,2048]{1,0:T(8,128)(2,1)S(1)}, bf16[16,2048]{1,0:T(8,128)(2,1)S(1)}, u32[]{:S(2)}, u32[]{:S(2)}) collective-permute-start(bf16[16,2048]{1,0:T(8,128)(2,1)S(1)} %get-tuple-element.1489), channel_id=1, source_target_pairs={{4,0},{8,4},{12,8},{16,12},{20,16},{24,20},{28,24},{32,28},{36,32}... | collective-permute-start | bytes 196616 | tf_op jit(solution)/shard_map/while/body/eval_jaxpr/ppermute | solution.py:39
  939.2 27.3 %collective-permute-start.3 = (bf16[16,2048]{1,0:T(8,128)(2,1)S(1)}, bf16[16,2048]{1,0:T(8,128)(2,1)S(1)}, u32[]{:S(2)}, u32[]{:S(2)}) collective-permute-start(bf16[16,2048]{1,0:T(8,128)(2,1)S(1)} %get-tuple-element.1489), channel_id=1, source_target_pairs={{4,0},{8,4},{12,8},{16,12},{20,16},{24,20},{28,24},{32,28},{36,32}... | collective-permute-start | bytes 196616 | tf_op jit(solution)/shard_map/while/body/eval_jaxpr/ppermute | solution.py:39
  968.5 14.6 %collective-permute-start = (f32[16,512]{1,0:T(8,128)S(1)}, f32[16,512]{1,0:T(8,128)S(1)}, u32[]{:S(2)}, u32[]{:S(2)}) collective-permute-start(f32[16,512]{1,0:T(8,128)S(1)} %get-tuple-element.1482), channel_id=1, source_target_pairs={{0,3},{1,0},{2,1},{3,2},{4,7},{5,4},{6,5},{7,6},{8,11},{9,8},{10,9... | collective-permute-start | bytes 98312 | tf_op jit(solution)/shard_map/while/body/eval_jaxpr/ppermute | solution.py:12
  990.5 21.4 %collective-permute-start.3 = (bf16[16,2048]{1,0:T(8,128)(2,1)S(1)}, bf16[16,2048]{1,0:T(8,128)(2,1)S(1)}, u32[]{:S(2)}, u32[]{:S(2)}) collective-permute-start(bf16[16,2048]{1,0:T(8,128)(2,1)S(1)} %get-tuple-element.1489), channel_id=1, source_target_pairs={{4,0},{8,4},{12,8},{16,12},{20,16},{24,20},{28,24},{32,28},{36,32}... | collective-permute-start | bytes 196616 | tf_op jit(solution)/shard_map/while/body/eval_jaxpr/ppermute | solution.py:39
  1034.2 21.2 %collective-permute-start.3 = (bf16[16,2048]{1,0:T(8,128)(2,1)S(1)}, bf16[16,2048]{1,0:T(8,128)(2,1)S(1)}, u32[]{:S(2)}, u32[]{:S(2)}) collective-permute-start(bf16[16,2048]{1,0:T(8,128)(2,1)S(1)} %get-tuple-element.1489), channel_id=1, source_target_pairs={{4,0},{8,4},{12,8},{16,12},{20,16},{24,20},{28,24},{32,28},{36,32}... | collective-permute-start | bytes 196616 | tf_op jit(solution)/shard_map/while/body/eval_jaxpr/ppermute | solution.py:39
  1057.4 14.4 %collective-permute-start = (f32[16,512]{1,0:T(8,128)S(1)}, f32[16,512]{1,0:T(8,128)S(1)}, u32[]{:S(2)}, u32[]{:S(2)}) collective-permute-start(f32[16,512]{1,0:T(8,128)S(1)} %get-tuple-element.1482), channel_id=1, source_target_pairs={{0,3},{1,0},{2,1},{3,2},{4,7},{5,4},{6,5},{7,6},{8,11},{9,8},{10,9... | collective-permute-start | bytes 98312 | tf_op jit(solution)/shard_map/while/body/eval_jaxpr/ppermute | solution.py:12
  1080.2 20.2 %collective-permute-start.3 = (bf16[16,2048]{1,0:T(8,128)(2,1)S(1)}, bf16[16,2048]{1,0:T(8,128)(2,1)S(1)}, u32[]{:S(2)}, u32[]{:S(2)}) collective-permute-start(bf16[16,2048]{1,0:T(8,128)(2,1)S(1)} %get-tuple-element.1489), channel_id=1, source_target_pairs={{4,0},{8,4},{12,8},{16,12},{20,16},{24,20},{28,24},{32,28},{36,32}... | collective-permute-start | bytes 196616 | tf_op jit(solution)/shard_map/while/body/eval_jaxpr/ppermute | solution.py:39
  1126.4 17.9 %collective-permute-start.3 = (bf16[16,2048]{1,0:T(8,128)(2,1)S(1)}, bf16[16,2048]{1,0:T(8,128)(2,1)S(1)}, u32[]{:S(2)}, u32[]{:S(2)}) collective-permute-start(bf16[16,2048]{1,0:T(8,128)(2,1)S(1)} %get-tuple-element.1489), channel_id=1, source_target_pairs={{4,0},{8,4},{12,8},{16,12},{20,16},{24,20},{28,24},{32,28},{36,32}... | collective-permute-start | bytes 196616 | tf_op jit(solution)/shard_map/while/body/eval_jaxpr/ppermute | solution.py:39
  1146.3 14.4 %collective-permute-start = (f32[16,512]{1,0:T(8,128)S(1)}, f32[16,512]{1,0:T(8,128)S(1)}, u32[]{:S(2)}, u32[]{:S(2)}) collective-permute-start(f32[16,512]{1,0:T(8,128)S(1)} %get-tuple-element.1482), channel_id=1, source_target_pairs={{0,3},{1,0},{2,1},{3,2},{4,7},{5,4},{6,5},{7,6},{8,11},{9,8},{10,9... | collective-permute-start | bytes 98312 | tf_op jit(solution)/shard_map/while/body/eval_jaxpr/ppermute | solution.py:12
  1224.8 14.6 %collective-permute-start = (f32[16,512]{1,0:T(8,128)S(1)}, f32[16,512]{1,0:T(8,128)S(1)}, u32[]{:S(2)}, u32[]{:S(2)}) collective-permute-start(f32[16,512]{1,0:T(8,128)S(1)} %get-tuple-element.1482), channel_id=1, source_target_pairs={{0,3},{1,0},{2,1},{3,2},{4,7},{5,4},{6,5},{7,6},{8,11},{9,8},{10,9... | collective-permute-start | bytes 98312 | tf_op jit(solution)/shard_map/while/body/eval_jaxpr/ppermute | solution.py:12
  1293.5 14.7 %collective-permute-start = (f32[16,512]{1,0:T(8,128)S(1)}, f32[16,512]{1,0:T(8,128)S(1)}, u32[]{:S(2)}, u32[]{:S(2)}) collective-permute-start(f32[16,512]{1,0:T(8,128)S(1)} %get-tuple-element.1482), channel_id=1, source_target_pairs={{0,3},{1,0},{2,1},{3,2},{4,7},{5,4},{6,5},{7,6},{8,11},{9,8},{10,9... | collective-permute-start | bytes 98312 | tf_op jit(solution)/shard_map/while/body/eval_jaxpr/ppermute | solution.py:12
  (116 other events, 2061.9 us)
Sparse Core Ops, SparseCore 0:
  24.9 26.1 all-gather.1
